TPU v7x, 256 devices: a whole 4x4x8 slice. The times are simulated.
256 devices in a mesh: dom: 8 (over y, x_lo), pix: 32 (over x_hi, z, core).
Axes of the slice: x: 4 (x_hi: 2, x_lo: 2; x = x_hi * 2 + x_lo), y: 4, z: 8, core: 2. Of those that a mesh axis runs over, the one named last changes fastest.
Arguments:
- images: bfloat16 [8192, 2, 32768], P('dom', None, 'pix'), may hold values from -6 to 6
- slices: bfloat16 [8, 256, 2, 32768], P('dom', None, None, 'pix'), may hold values from -6 to 6
- class_of: int32 [8192, 1], P('dom'), may hold values from 0 to 7, as said below
- pose_of: int32 [8192], P('dom'), may hold values from 0 to 255, as said below
- group_of: int32 [8192], P('dom'), may hold values from 0 to 63
- defocus: bfloat16 [8192], P('dom'), may hold values from 0.5 to 1.5
- slot_class: int32 [8], replicated, may hold values from 0 to 7, each once
Outputs:
- whitened: float32 [64, 12], replicated
- defocus_score: float32 [8192], P('dom')
Inputs may be any that keep to these rules, and one draw needn't show every extreme that they name: Slot j of slices holds the projected slices of class slot_class[j]; every class stands in exactly one slot. `class_of`: among the 1024 particles of one device at most 192 have the same class; on every device one or two classes have exactly 192. `pose_of`: among one device's particles of one class, a pose is used a second time only after all 256 poses have been used.
All inputs are finite; a program needn't handle non-finite values.
Results may differ from a plain program's by a relative error of at most 0.0003.
Values may be sent and summed in bfloat16 or wider, within the bound.
No kernel may reach another device: no remote copies, remote signals or barrier semaphores. Data moves between devices by JAX's collectives and lax.ppermute only.
A program may use at most 128 MiB of HBM per device.

v0:
```python
import math

import jax
import jax.numpy as jnp
from jax import lax
from jax.sharding import PartitionSpec as P

BOX = 256
GROUPS = 64
ZERN = 12


PHASE_GAIN = 40.0
RIDGE = 1.0


def broadcast(block, axis, owner):
    block = jnp.where(lax.axis_index(axis) == owner, block, jnp.zeros_like(block))
    return lax.psum(block, axis)


def pixel_grid(pix_start, pix_count):
    pixel_index = pix_start + jnp.arange(pix_count, dtype=jnp.int32)
    half_box = BOX // 2
    radial_scale = math.sqrt(2.0) / BOX
    freq_x = (pixel_index % half_box).astype(jnp.float32) * radial_scale
    freq_y = (pixel_index // half_box - half_box).astype(jnp.float32) * radial_scale
    return (freq_x, freq_y)


def zernike(freq_x, freq_y):
    radius_sq = freq_x * freq_x + freq_y * freq_y
    real_one, imag_one = (freq_x, freq_y)
    real_two = freq_x * freq_x - freq_y * freq_y
    imag_two = 2.0 * freq_x * freq_y
    real_three = real_two * real_one - imag_two * imag_one
    imag_three = real_two * imag_one + imag_two * real_one
    real_five = real_three * real_two - imag_three * imag_two
    imag_five = real_three * imag_two + imag_three * real_two
    radial_three = 3.0 * radius_sq - 2.0
    radial_five = 10.0 * radius_sq * radius_sq - 12.0 * radius_sq + 3.0
    radial_outer = 5.0 * radius_sq - 4.0
    return jnp.stack(
        [
            real_one,
            imag_one,
            radial_three * real_one,
            radial_three * imag_one,
            radial_five * real_one,
            radial_five * imag_one,
            real_three,
            imag_three,
            radial_outer * real_three,
            radial_outer * imag_three,
            real_five,
            imag_five,
        ]
    )


def particle_terms(row_block, projected, defocus_rows, radius_sq):
    phase_chi = PHASE_GAIN * defocus_rows.astype(jnp.float32)[:, None] * radius_sq[None, :]
    ctf_value = -jnp.sin(phase_chi)
    ctf_slope = -PHASE_GAIN * radius_sq[None, :] * jnp.cos(phase_chi)
    proj_real = projected[:, 0, :].astype(jnp.float32)
    proj_imag = projected[:, 1, :].astype(jnp.float32)
    image_real = row_block[:, 0, :].astype(jnp.float32)
    image_imag = row_block[:, 1, :].astype(jnp.float32)
    pred_real = ctf_value * proj_real
    pred_imag = ctf_value * proj_imag
    pred_power = pred_real * pred_real + pred_imag * pred_imag
    cross_term = pred_real * image_imag - pred_imag * image_real
    gradient = jnp.sum(
        ctf_slope * (proj_real * (pred_real - image_real) + proj_imag * (pred_imag - image_imag)),
        axis=1,
    )
    curvature = jnp.sum(
        ctf_slope * ctf_slope * (proj_real * proj_real + proj_imag * proj_imag), axis=1
    )
    return (pred_power, cross_term, gradient, curvature)


def contract(group_sums, zernike_basis, pix_count):
    pair_table = (zernike_basis[:, None, :] * zernike_basis[None, :, :]).reshape(
        ZERN * ZERN, pix_count
    )
    power_sums = group_sums[:, :pix_count]
    cross_sums = group_sums[:, pix_count:]
    normal_flat = jnp.dot(power_sums, pair_table.T, precision=lax.Precision.HIGHEST)
    right_side = jnp.dot(cross_sums, zernike_basis.T, precision=lax.Precision.HIGHEST)
    return (normal_flat, right_side)


def whiten(normal_flat, right_side):
    normal = normal_flat.reshape(GROUPS, ZERN, ZERN) + RIDGE * jnp.eye(ZERN, dtype=jnp.float32)
    factor = jnp.linalg.cholesky(normal)
    solved = lax.linalg.triangular_solve(factor, right_side[:, :, None], left_side=True, lower=True)
    return solved[:, :, 0]


def group_total(group_hot, pred_power, cross_term):
    joined = jnp.concatenate([pred_power, cross_term], axis=1)
    return lax.dot_general(
        group_hot, joined, (((0,), (0,)), ((), ())), precision=lax.Precision.HIGHEST
    )


def local(images, slices, class_of, pose_of, group_of, defocus, slot_class):
    part_rows = images.shape[0]
    pix_count = images.shape[2]
    pose_total = slices.shape[1]
    dom_count = lax.axis_size("dom")
    class_col = class_of[:, 0]
    freq_x, freq_y = pixel_grid(lax.axis_index("pix") * pix_count, pix_count)
    radius_sq = freq_x * freq_x + freq_y * freq_y
    zernike_basis = zernike(freq_x, freq_y)
    flat_slices = slices.reshape(pose_total, 2 * pix_count)
    pose_ids = jnp.arange(pose_total, dtype=jnp.int32)
    group_ids = jnp.arange(GROUPS, dtype=jnp.int32)

    def pick_rows(poses_wanted, wanted, stack_rows):
        pose_hot = ((poses_wanted[:, None] == pose_ids[None, :]) & wanted[:, None]).astype(
            jnp.bfloat16
        )
        return jnp.dot(pose_hot, stack_rows, preferred_element_type=jnp.float32).astype(
            jnp.bfloat16
        )

    empty_rows = jnp.zeros((part_rows, 2 * pix_count), jnp.bfloat16)

    def add_slot(slot_index, accumulated):
        stack_rows = broadcast(flat_slices, "dom", slot_index)
        return accumulated + pick_rows(pose_of, class_col == slot_class[slot_index], stack_rows)

    projected = lax.fori_loop(0, dom_count, add_slot, empty_rows)
    projected = projected.reshape(part_rows, 2, pix_count)
    pred_power, cross_term, gradient, curvature = particle_terms(
        images, projected, defocus, radius_sq
    )
    group_hot = (group_of[:, None] == group_ids[None, :]).astype(jnp.float32)
    group_sums = group_total(group_hot, pred_power, cross_term)
    gradient, curvature = lax.psum((gradient, curvature), "pix")
    defocus_score = -gradient * lax.rsqrt(curvature + 1e-06)
    group_sums = lax.psum(group_sums, "dom")
    normal_flat, right_side = contract(group_sums, zernike_basis, pix_count)
    normal_flat, right_side = lax.psum((normal_flat, right_side), "pix")
    whitened = whiten(normal_flat, right_side)
    return (whitened, defocus_score)


def solution(mesh):
    return jax.shard_map(
        local,
        mesh=mesh,
        in_specs=(
            P("dom", None, "pix"),
            P("dom", None, None, "pix"),
            P("dom", None),
            P("dom"),
            P("dom"),
            P("dom"),
            P(),
        ),
        out_specs=(P(), P("dom")),
        check_vma=False,
    )
```

profile of v0, /device:TPU:1, one launch (start us, length us, event | category | flops | bytes accessed | tf_op | source)
XLA Modules:
  0.0 1115.3 jit_solution(10211409934519042154)
XLA Ops:
  8.7 1.5 copy.67
  10.2 750.5 %while.14 = (s32[]{:T(128)}, bf16[1024,2048]{1,0:T(8,128)(2,1)}, s32[1024]{0:T(1024)}, s32[8]{0:T(128)}, s32[1024]{0:T(1024)}, /*index=5*/bf16[256,2048]{1,0:T(8...) while((s32[]{:T(128)}, bf16[1024,2048]{1,0:T(8,128)(2,1)}, s32[1024]{0:T(1024)}, ...), condition=%wide.region_2.3_spmd.clone, body=%wide.region_0.2_spmd.clone.sunk | while | flops 1081607168 | bytes 17836248 | solution.py:135
  12.7 1.3 broadcast_compare_fusion.2
  14.0 85.5 %all-reduce.6.cloned.1.call-done = bf16[256,2048]{1,0:T(8,128)(2,1)} async-done(((bf16[256,2048]{1,0:T(8,128)(2,1)}), bf16[256,2048]{1,0:T(8,128)(2,1)}) %all-reduce.6.cloned.1.call-update) | async-done | bytes 1048592 | tf_op jit(solution)/shard_map/while/body/eval_jaxpr/psum | solution.py:19
  99.5 4.6 select_add_fusion.2
  107.9 84.9 %all-reduce.6.cloned.1.call-done = bf16[256,2048]{1,0:T(8,128)(2,1)} async-done(((bf16[256,2048]{1,0:T(8,128)(2,1)}), bf16[256,2048]{1,0:T(8,128)(2,1)}) %all-reduce.6.cloned.1.call-update) | async-done | bytes 1048592 | tf_op jit(solution)/shard_map/while/body/eval_jaxpr/psum | solution.py:19
  192.8 5.3 select_add_fusion.2
  200.4 1.3 broadcast_compare_fusion.2
  201.8 85.0 %all-reduce.6.cloned.1.call-done = bf16[256,2048]{1,0:T(8,128)(2,1)} async-done(((bf16[256,2048]{1,0:T(8,128)(2,1)}), bf16[256,2048]{1,0:T(8,128)(2,1)}) %all-reduce.6.cloned.1.call-update) | async-done | bytes 1048592 | tf_op jit(solution)/shard_map/while/body/eval_jaxpr/psum | solution.py:19
  286.7 5.3 select_add_fusion.2
  295.7 84.6 %all-reduce.6.cloned.1.call-done = bf16[256,2048]{1,0:T(8,128)(2,1)} async-done(((bf16[256,2048]{1,0:T(8,128)(2,1)}), bf16[256,2048]{1,0:T(8,128)(2,1)}) %all-reduce.6.cloned.1.call-update) | async-done | bytes 1048592 | tf_op jit(solution)/shard_map/while/body/eval_jaxpr/psum | solution.py:19
  380.4 5.3 select_add_fusion.2
  389.3 84.6 %all-reduce.6.cloned.1.call-done = bf16[256,2048]{1,0:T(8,128)(2,1)} async-done(((bf16[256,2048]{1,0:T(8,128)(2,1)}), bf16[256,2048]{1,0:T(8,128)(2,1)}) %all-reduce.6.cloned.1.call-update) | async-done | bytes 1048592 | tf_op jit(solution)/shard_map/while/body/eval_jaxpr/psum | solution.py:19
  474.0 5.3 select_add_fusion.2
  483.0 84.6 %all-reduce.6.cloned.1.call-done = bf16[256,2048]{1,0:T(8,128)(2,1)} async-done(((bf16[256,2048]{1,0:T(8,128)(2,1)}), bf16[256,2048]{1,0:T(8,128)(2,1)}) %all-reduce.6.cloned.1.call-update) | async-done | bytes 1048592 | tf_op jit(solution)/shard_map/while/body/eval_jaxpr/psum | solution.py:19
  567.6 5.3 select_add_fusion.2
  576.6 84.9 %all-reduce.6.cloned.1.call-done = bf16[256,2048]{1,0:T(8,128)(2,1)} async-done(((bf16[256,2048]{1,0:T(8,128)(2,1)}), bf16[256,2048]{1,0:T(8,128)(2,1)}) %all-reduce.6.cloned.1.call-update) | async-done | bytes 1048592 | tf_op jit(solution)/shard_map/while/body/eval_jaxpr/psum | solution.py:19
  661.5 5.3 select_add_fusion.2
  670.5 84.9 %all-reduce.6.cloned.1.call-done = bf16[256,2048]{1,0:T(8,128)(2,1)} async-done(((bf16[256,2048]{1,0:T(8,128)(2,1)}), bf16[256,2048]{1,0:T(8,128)(2,1)}) %all-reduce.6.cloned.1.call-update) | async-done | bytes 1048592 | tf_op jit(solution)/shard_map/while/body/eval_jaxpr/psum | solution.py:19
  755.4 5.3 select_add_fusion.2
  760.7 6.4 copy.46
  767.1 10.0 fusion.58
  777.1 9.0 copy.64
  786.1 5.2 fusion.25
  791.3 5.3 copy.49
  796.6 21.2 %fusion.20 = (f32[1024]{0:T(1024)S(1)}, f32[1024]{0:T(1024)S(1)}, f32[1024,1024]{0,1:T(8,128)S(1)}, f32[1024,1024]{0,1:T(8,128)S(1)}) fusion(f32[1024,1024]{0,1:T(8,128)} %copy.49, bf16[1024,1,1024]{0,2,1:T(8,128)(2,1)S(1)} %copy.64, f32[1024]{0:T(1024)S(1)} %get-tuple-element.173, f32[1024]{0:T(1024)S(1)} %get-tuple-element.172, ...), kind=kLoop, calls=%fused_computation.32 | loop fusion | flops 28309504 | bytes 18894848 | tf_op jit(solution)/shard_map/reduce_sum | solution.py:73
  817.8 5.4 fusion.6
  824.0 77.9 %all-reduce.4.cloned.1.call-done = f32[64,2048]{1,0:T(8,128)} async-done(((f32[64,2048]{1,0:T(8,128)}), f32[64,2048]{1,0:T(8,128)}) %all-reduce.4.cloned.1.call-update) | async-done | bytes 524304 | tf_op jit(solution)/shard_map/psum | solution.py:144
  901.9 1.6 fusion.30
  904.7 129.0 %all-reduce = (f32[64,12,12]{0,1,2:T(8,128)S(1)}, f32[64,12]{0,1:T(8,128)S(1)}, f32[1024]{0:T(1024)S(1)}, f32[1024]{0:T(1024)S(1)}) all-reduce(f32[64,12,12]{0,1,2:T(8,128)S(1)} %copy.51, f32[64,12]{0,1:T(8,128)S(1)} %fusion.28, f32[1024]{0:T(1024)S(1)} %get-tuple-element.151, ...), channel_id=1, replica_groups=mesh['dom'=8,'pix'=32] {'pix'}, use_global_device_ids=true, to_apply=%region_4.5 | all-reduce | flops 12032 | bytes 96256 | tf_op jit(solution)/shard_map/psum | solution.py:146
  1034.2 70.4 %custom-call.7 = f32[64,12,12]{2,1,0:T(8,128)S(1)} custom-call(f32[64,12,12]{2,1,0:T(8,128)S(1)} %broadcast_multiply_fusion.1), custom_call_target="Cholesky" | custom-call | tf_op jit(solution)/shard_map/jit(cholesky)/cholesky | solution.py:96
  1105.0 1.6 custom-call.8
  (71 shorter events, 31.8 us)
Async XLA Ops:
  10.2 89.3 %all-reduce.6.cloned.1.call-start = ((), (), s32[]{:S(2)}) async-start(), calls=%async_computation.1 | async-start | bytes 2097152 | tf_op jit(solution)/shard_map/while/body/eval_jaxpr/psum | solution.py:19
  104.1 88.7 %all-reduce.6.cloned.1.call-start = ((), (), s32[]{:S(2)}) async-start(), calls=%async_computation.1 | async-start | bytes 2097152 | tf_op jit(solution)/shard_map/while/body/eval_jaxpr/psum | solution.py:19
  198.1 88.7 %all-reduce.6.cloned.1.call-start = ((), (), s32[]{:S(2)}) async-start(), calls=%async_computation.1 | async-start | bytes 2097152 | tf_op jit(solution)/shard_map/while/body/eval_jaxpr/psum | solution.py:19
  292.0 88.3 %all-reduce.6.cloned.1.call-start = ((), (), s32[]{:S(2)}) async-start(), calls=%async_computation.1 | async-start | bytes 2097152 | tf_op jit(solution)/shard_map/while/body/eval_jaxpr/psum | solution.py:19
  385.6 88.3 %all-reduce.6.cloned.1.call-start = ((), (), s32[]{:S(2)}) async-start(), calls=%async_computation.1 | async-start | bytes 2097152 | tf_op jit(solution)/shard_map/while/body/eval_jaxpr/psum | solution.py:19
  479.2 88.3 %all-reduce.6.cloned.1.call-start = ((), (), s32[]{:S(2)}) async-start(), calls=%async_computation.1 | async-start | bytes 2097152 | tf_op jit(solution)/shard_map/while/body/eval_jaxpr/psum | solution.py:19
  572.8 88.7 %all-reduce.6.cloned.1.call-start = ((), (), s32[]{:S(2)}) async-start(), calls=%async_computation.1 | async-start | bytes 2097152 | tf_op jit(solution)/shard_map/while/body/eval_jaxpr/psum | solution.py:19
  666.8 88.7 %all-reduce.6.cloned.1.call-start = ((), (), s32[]{:S(2)}) async-start(), calls=%async_computation.1 | async-start | bytes 2097152 | tf_op jit(solution)/shard_map/while/body/eval_jaxpr/psum | solution.py:19
  760.7 141.2 %all-reduce.4.cloned.1.call-start = ((), (), s32[]{:S(2)}) async-start(), calls=%async_computation | async-start | bytes 1048576 | tf_op jit(solution)/shard_map/psum | solution.py:144
  796.6 21.2 %copy-start = (s32[1024]{0:T(1024)S(1)}, s32[1024]{0:T(1024)}, u32[]{:S(2)}) copy-start(s32[1024]{0:T(1024)} %param.13) | copy-start | bytes 12292
Sparse Core Ops, SparseCore 0:
  13.9 85.5 all-reduce.5
  107.8 84.9 all-reduce.5
  201.7 84.9 all-reduce.5
  295.4 84.9 all-reduce.5
  389.0 84.9 all-reduce.5
  482.6 84.9 all-reduce.5
  576.5 84.9 all-reduce.5
  670.4 84.9 all-reduce.5
Sparse Core Ops, SparseCore 1:
  823.3 78.5 all-reduce.3
where the time goes:
time: 1120 us
  waiting for transfers between devices  757 us (68%)
  blocking collectives  129 us (12%)
  other arithmetic  121 us (11%)
  matrix products  49.7 us (4%)
  local copies, waits for them, and re-layouts  43 us (4%)
  between operations  15.6 us (1%)
    psum x8, waiting for transfers between devices, broadcast(): return lax.psum(block, axis)  679 us
    psum x1, blocking collectives, local(): normal_flat, right_side = lax.psum((normal_flat, right_side), 'pix')  129 us
    psum x1, waiting for transfers between devices, local(): group_sums = lax.psum(group_sums, 'dom')  77.9 us
    another operation x4, other arithmetic, whiten(): factor = jnp.linalg.cholesky(normal)  70.5 us
    dot_general x8, matrix products, pick_rows(): jnp.dot(pose_hot, stack_rows, preferred_element_type=jnp.float32)  41.5 us
  transfers between devices with their start and end apart: 9, of which 9 were waited for; matrix products, arithmetic and copies ran while one was open for 2% of the time, Pallas kernels for 0%

commit v1 on v0

v1 whole, which is shorter than its diff:
```python
import functools
import math

import jax
import jax.numpy as jnp
from jax import lax
from jax.experimental import pallas as pl
from jax.experimental.pallas import tpu as pltpu
from jax.sharding import PartitionSpec as P

BOX = 256
GROUPS = 64
ZERN = 12
PAIRS = ZERN * (ZERN + 1) // 2
PHASE_GAIN = 40.0
RIDGE = 1.0

CHUNKS = 4
ROWS = 256
MOMENTS = 96
RIGHT_AT = 80

SIN_POLY = (3.141592580044675, -5.167706878922935, 2.5500313772212047, -0.5980451737557255, 0.07722012821305138)
COS_POLY = (0.9999999534415752, -4.934792857330457, 4.058411894717311, -1.3318800570964462, 0.2196966127309024)

X_SWAP = [(d, d ^ 1) for d in range(8)]
Y_UP = [(d, (d + 2) % 8) for d in range(8)]
Y_DOWN = [(d, (d - 2) % 8) for d in range(8)]
CORE_SWAP = [(p, p ^ 1) for p in range(32)]
CORE_GROUPS = [[2 * m + c for m in range(16)] for c in range(2)]

F32 = jnp.float32
BF16 = jnp.bfloat16
SMEM = pl.BlockSpec(memory_space=pltpu.SMEM)
VMEM = pl.BlockSpec(memory_space=pltpu.VMEM)


def params():
    return pltpu.CompilerParams(vmem_limit_bytes=40 * 1024 * 1024)


def horner(coeffs, z):
    acc = jnp.full_like(z, coeffs[-1])
    for c in coeffs[-2::-1]:
        acc = acc * z + c
    return acc


def hot_kernel(place, slot_class, class_ref, pose_ref, hot_ref):
    y0 = place[0] >> 1
    x0 = place[0] & 1
    cls = class_ref[...]
    block = jnp.zeros_like(cls)
    for slot in range(8):
        near = ((((slot >> 1) - y0) & 3) << 1) | ((slot & 1) ^ x0)
        block = jnp.where(cls == slot_class[slot], near, block)
    row = block * 256 + pose_ref[...]
    col = lax.broadcasted_iota(jnp.int32, hot_ref.shape, 1)
    hot_ref[...] = jnp.where(col == row, 1.0, 0.0).astype(BF16)


def hot_rows(place, slot_class, class_of, pose_of):
    parts = class_of.shape[0]
    return pl.pallas_call(
        hot_kernel,
        grid=(parts // ROWS,),
        in_specs=[
            SMEM,
            SMEM,
            pl.BlockSpec((ROWS, 1), lambda i: (i, 0)),
            pl.BlockSpec((ROWS, 1), lambda i: (i, 0)),
        ],
        out_specs=pl.BlockSpec((ROWS, 2048), lambda i: (i, 0)),
        out_shape=jax.ShapeDtypeStruct((parts, 2048), BF16),
        compiler_params=params(),
        name="hot_rows",
    )(place, slot_class, class_of, pose_of)


def pixel_grid(first, count):
    index = first + lax.broadcasted_iota(jnp.int32, (1, count), 1)
    scale = math.sqrt(2.0) / BOX
    freq_x = (index & (BOX // 2 - 1)).astype(F32) * scale
    freq_y = ((index >> 7) - BOX // 2).astype(F32) * scale
    return freq_x, freq_y


def zernike_rows(freq_x, freq_y):
    q = freq_x * freq_x + freq_y * freq_y
    re1, im1 = freq_x, freq_y
    re2 = freq_x * freq_x - freq_y * freq_y
    im2 = 2.0 * freq_x * freq_y
    re3 = re2 * re1 - im2 * im1
    im3 = re2 * im1 + im2 * re1
    re5 = re3 * re2 - im3 * im2
    im5 = re3 * im2 + im3 * re2
    r3 = 3.0 * q - 2.0
    r5 = 10.0 * q * q - 12.0 * q + 3.0
    ro = 5.0 * q - 4.0
    return [re1, im1, r3 * re1, r3 * im1, r5 * re1, r5 * im1, re3, im3, ro * re3, ro * im3, re5, im5]


def chunk_kernel(fill, first, hot_ref, re_ref, im_ref, defocus_ref, group_ref, *rest):
    pieces = rest[: -6]
    moment_ref, grad_ref, table, sums, basis, pairs = rest[-6:]
    step = pl.program_id(0)
    count = re_ref.shape[1]
    freq_x, freq_y = pixel_grid(first[0], count)
    q = freq_x * freq_x + freq_y * freq_y

    @pl.when(step == 0)
    def _():
        for piece, src, dst, rows in fill:
            table[dst : dst + rows, :] = pieces[piece][src : src + rows, :]
        sums[...] = jnp.zeros_like(sums)

    proj = jnp.dot(hot_ref[...], table[...], preferred_element_type=F32)
    proj_re = proj[:, :count]
    proj_im = proj[:, count:]
    image_re = re_ref[...].astype(F32)
    image_im = im_ref[...].astype(F32)

    turns = (defocus_ref[...] * (PHASE_GAIN / (2.0 * math.pi))) * q
    rest_turn = turns - jnp.floor(turns + 0.5)
    z = rest_turn * rest_turn
    s = rest_turn * horner(SIN_POLY, z)
    c = horner(COS_POLY, z)
    s2 = s + s
    sin_phi = s2 * c
    cos_phi = 1.0 - s2 * s

    power = proj_re * proj_re + proj_im * proj_im
    along = proj_re * image_re + proj_im * image_im
    across = proj_im * image_re - proj_re * image_im
    weight = (PHASE_GAIN * q) * cos_phi
    sp = sin_phi * power
    grad = weight * (sp + along)
    curv = weight * weight * power
    pred_power = sin_phi * sp
    cross = sin_phi * across

    cross_hi = cross.astype(BF16)
    cross_lo = (cross - cross_hi.astype(F32)).astype(BF16)
    group_hot = jnp.where(
        lax.broadcasted_iota(jnp.int32, (GROUPS, ROWS), 0) == group_ref[...], 1.0, 0.0
    ).astype(BF16)
    sums[:, 0:count] += jnp.dot(group_hot, pred_power.astype(BF16), preferred_element_type=F32)
    sums[:, count:] += jnp.dot(group_hot, cross_hi, preferred_element_type=F32) + jnp.dot(
        group_hot, cross_lo, preferred_element_type=F32
    )

    def lanes(v):
        return sum(v[:, 128 * i : 128 * i + 128] for i in range(count // 128))

    grad_ref[0:1, :] = jnp.sum(lanes(grad).T, axis=0, keepdims=True)
    grad_ref[1:2, :] = jnp.sum(lanes(curv).T, axis=0, keepdims=True)

    @pl.when(step == pl.num_programs(0) - 1)
    def _():
        basis[...] = jnp.zeros_like(basis)
        for j, row in enumerate(zernike_rows(freq_x, freq_y)):
            basis[j : j + 1, :] = row
        pairs[72:80, :] = jnp.zeros((8, count), F32)
        at = 0
        for j in range(ZERN):
            pairs[at : at + ZERN - j, :] = basis[j : j + 1, :] * basis[j:ZERN, :]
            at += ZERN - j
        nt = (((1,), (1,)), ((), ()))
        moment_ref[0:RIGHT_AT, :] = lax.dot_general(
            pairs[...], sums[:, :count], nt, precision=lax.Precision.HIGHEST, preferred_element_type=F32
        )
        moment_ref[RIGHT_AT:, :] = lax.dot_general(
            basis[...], sums[:, count:], nt, precision=lax.Precision.HIGHEST, preferred_element_type=F32
        )


def chunk_terms(chunk, fill, first, hot, images, defocus_col, group_row, pieces):
    parts = hot.shape[0]
    count = images.shape[1] // (2 * CHUNKS)
    return pl.pallas_call(
        functools.partial(chunk_kernel, fill),
        grid=(parts // ROWS,),
        in_specs=[
            SMEM,
            pl.BlockSpec((ROWS, 2048), lambda i: (i, 0)),
            pl.BlockSpec((ROWS, count), lambda i: (i, chunk)),
            pl.BlockSpec((ROWS, count), lambda i: (i, CHUNKS + chunk)),
            pl.BlockSpec((ROWS, 1), lambda i: (i, 0)),
            pl.BlockSpec((1, ROWS), lambda i: (0, i)),
        ]
        + [pl.BlockSpec(p.shape, lambda i: (0, 0)) for p in pieces],
        out_specs=[
            pl.BlockSpec((MOMENTS, GROUPS), lambda i: (0, 0)),
            pl.BlockSpec((2, ROWS), lambda i: (0, i)),
        ],
        out_shape=[
            jax.ShapeDtypeStruct((MOMENTS, GROUPS), F32),
            jax.ShapeDtypeStruct((2, parts), F32),
        ],
        scratch_shapes=[
            pltpu.VMEM((2048, 2 * count), BF16),
            pltpu.VMEM((GROUPS, 2 * count), F32),
            pltpu.VMEM((16, count), F32),
            pltpu.VMEM((RIGHT_AT, count), F32),
        ],
        compiler_params=params(),
        cost_estimate=pl.CostEstimate(
            flops=2 * parts * 2048 * 2 * count, bytes_accessed=8 * 1024 * 1024, transcendentals=0
        ),
        name="chunk_terms",
    )(first, hot, images, images, defocus_col, group_row, *pieces)


def pack_kernel(core, *refs):
    keep_ref, send_ref, full = refs[-3:]
    moments = sum(r[...] for r in refs[:CHUNKS])
    grads = sum(r[...] for r in refs[CHUNKS : 2 * CHUNKS])
    half = MOMENTS // 2
    packed = jnp.concatenate([moments[:half], moments[half:]], axis=1)
    for h in range(2):
        full[32 * h : 32 * h + 24, :] = packed[24 * h : 24 * h + 24]
        for r in range(4):
            at = 512 * h + 128 * r
            full[32 * h + 24 + r : 32 * h + 25 + r, :] = grads[0:1, at : at + 128]
            full[32 * h + 28 + r : 32 * h + 29 + r, :] = grads[1:2, at : at + 128]
    keep_ref[...] = full[pl.ds(pl.multiple_of(core[0] * 32, 32), 32), :]
    send_ref[...] = full[pl.ds(pl.multiple_of((1 - core[0]) * 32, 32), 32), :]


def spread_dom_kernel(a_ref, b_ref, out_ref, grad_ref):
    total = a_ref[...] + b_ref[...]
    grad_ref[...] = total[24:]
    for i in range(8):
        out_ref[i] = total[:24]


def spread_pix_kernel(in_ref, grad_ref, out_ref):
    total = in_ref[0]
    for i in range(1, 8):
        total = total + in_ref[i]
    grad = grad_ref[...]
    for i in range(16):
        out_ref[i, 0:24] = total
        out_ref[i, 24:32] = grad


def total_kernel(in_ref, out_ref):
    total = in_ref[0]
    for i in range(1, 16):
        total = total + in_ref[i]
    out_ref[...] = total


def whiten_kernel(core, own_ref, other_ref, white_ref, score_ref, both, rows):
    both[pl.ds(pl.multiple_of(core[0] * 32, 32), 32), :] = own_ref[...]
    both[pl.ds(pl.multiple_of((1 - core[0]) * 32, 32), 32), :] = other_ref[...]
    low = jnp.concatenate([both[0:24, :], both[32:56, :]], axis=0)
    moments = jnp.concatenate([low[:, :GROUPS], low[:, GROUPS:]], axis=0)
    at = 0
    rows[...] = jnp.zeros_like(rows)
    for j in range(ZERN):
        rows[j, j:ZERN, :] = moments[at : at + ZERN - j]
        at += ZERN - j
    right = moments[RIGHT_AT : RIGHT_AT + 16]
    line = [rows[j] for j in range(ZERN)]
    lane_row = lax.broadcasted_iota(jnp.int32, (16, GROUPS), 0)
    done = jnp.zeros((16, GROUPS), F32)
    for j in range(ZERN):
        inv = lax.rsqrt(line[j][j : j + 1] + RIDGE)
        col = line[j] * inv
        value = right[j : j + 1] * inv
        done = jnp.where(lane_row == j, value, done)
        right = right - col * value
        for i in range(j + 1, ZERN):
            line[i] = line[i] - col[i : i + 1] * col
    white_ref[...] = done.T[:, :ZERN]
    for h in range(2):
        grad = both[32 * h + 24 : 32 * h + 28, :]
        curv = both[32 * h + 28 : 32 * h + 32, :]
        score_ref[4 * h : 4 * h + 4, :] = -grad * lax.rsqrt(curv + 1e-06)


def reduce_all(core, moments, grads):
    half = jax.ShapeDtypeStruct((32, 128), F32)
    keep, send = pl.pallas_call(
        pack_kernel,
        in_specs=[SMEM] + [VMEM] * (2 * CHUNKS),
        out_shape=[half, half],
        scratch_shapes=[pltpu.VMEM((64, 128), F32)],
        name="pack",
    )(core, *moments, *grads)
    other = lax.ppermute(send, "pix", CORE_SWAP)
    spread, grad = pl.pallas_call(
        spread_dom_kernel,
        out_shape=[jax.ShapeDtypeStruct((8, 24, 128), F32), jax.ShapeDtypeStruct((8, 128), F32)],
        name="spread_dom",
    )(keep, other)
    spread = lax.all_to_all(spread, "dom", 0, 0)
    spread = pl.pallas_call(
        spread_pix_kernel,
        out_shape=jax.ShapeDtypeStruct((16, 32, 128), F32),
        name="spread_pix",
    )(spread, grad)
    spread = lax.all_to_all(spread, "pix", 0, 0, axis_index_groups=CORE_GROUPS)
    own = pl.pallas_call(total_kernel, out_shape=half, name="total")(spread)
    other = lax.ppermute(own, "pix", CORE_SWAP)
    white, score = pl.pallas_call(
        whiten_kernel,
        in_specs=[SMEM, VMEM, VMEM],
        out_shape=[
            jax.ShapeDtypeStruct((GROUPS, ZERN), F32),
            jax.ShapeDtypeStruct((8, 128), F32),
        ],
        scratch_shapes=[pltpu.VMEM((64, 128), F32), pltpu.VMEM((ZERN, 16, GROUPS), F32)],
        name="whiten",
    )(core, own, other)
    return white, score.reshape(-1)


def hop(block, perm):
    return lax.ppermute(block, "dom", perm)


FILL_X_FIRST = [(0, 0, 0, 512), (1, 0, 1536, 512), (2, 0, 512, 512), (3, 0, 1024, 256), (4, 0, 1280, 256)]
FILL_Y_FIRST = [(0, 0, 0, 256), (0, 256, 1536, 256), (0, 512, 512, 256), (0, 768, 1024, 256)] + [
    (1, 0, 256, 256),
    (1, 256, 1792, 256),
    (1, 512, 768, 256),
    (1, 768, 1280, 256),
]


def gather_x_first(own):
    pair = jnp.concatenate([own, hop(own, X_SWAP)], axis=0)
    below = hop(pair, Y_UP)
    above = hop(pair, Y_DOWN)
    far_0 = hop(below[:256], Y_UP)
    far_1 = hop(above[256:], Y_DOWN)
    return [pair, below, above, far_0, far_1]


def gather_y_first(own):
    below = hop(own, Y_UP)
    above = hop(own, Y_DOWN)
    far_0 = hop(below[:128], Y_UP)
    far_1 = hop(above[128:], Y_DOWN)
    column = jnp.concatenate([own, below, above, far_0, far_1], axis=0)
    return [column, hop(column, X_SWAP)]


def local(images, slices, class_of, pose_of, group_of, defocus, slot_class):
    parts, _, pix_count = images.shape
    poses = slices.shape[1]
    count = pix_count // CHUNKS
    dom_at = lax.axis_index("dom").astype(jnp.int32).reshape(1)
    pix_at = lax.axis_index("pix").astype(jnp.int32)
    core = (pix_at & 1).reshape(1)
    flat = slices.reshape(poses, 2 * pix_count)
    own = [
        jnp.concatenate(
            [flat[:, c * count : (c + 1) * count], flat[:, pix_count + c * count : pix_count + (c + 1) * count]],
            axis=1,
        )
        for c in range(CHUNKS)
    ]
    gathered = {0: gather_y_first(own[0]), 1: gather_x_first(own[1]), 2: gather_x_first(own[2]), 3: gather_y_first(own[3])}
    hot = hot_rows(dom_at, slot_class, class_of, pose_of[:, None])
    image_rows = images.reshape(parts, 2 * pix_count)
    defocus_col = defocus.astype(F32)[:, None]
    group_row = group_of[None, :]
    moments, grads = [], []
    for c in range(CHUNKS):
        fill = FILL_Y_FIRST if c in (0, 3) else FILL_X_FIRST
        first = (pix_at * pix_count + c * count).reshape(1)
        m, g = chunk_terms(c, fill, first, hot, image_rows, defocus_col, group_row, gathered[c])
        moments.append(m)
        grads.append(g)
    return reduce_all(core, moments, grads)


def solution(mesh):
    return jax.shard_map(
        local,
        mesh=mesh,
        in_specs=(
            P("dom", None, "pix"),
            P("dom", None, None, "pix"),
            P("dom", None),
            P("dom"),
            P("dom"),
            P("dom"),
            P(),
        ),
        out_specs=(P(), P("dom")),
        check_vma=False,
    )
```

time: 1120 us -> 146 us (0.13)
  waiting for transfers between devices: 757 us -> 22.2 us
  other arithmetic: 121 us -> 1.63 us
  blocking collectives: 129 us -> 29.3 us
  matrix products: 49.7 us -> 0 us
  Pallas kernels: 0 us -> 34.9 us
  starting transfers between devices: 0.06 us -> 30.5 us
  local copies, waits for them, and re-layouts: 43 us -> 25.3 us
  between operations: 15.6 us -> 0.99 us
    psum x9 -> x0, waiting for transfers between devices: 757 us -> none  [the longest x8 679 us: broadcast(): return lax.psum(block, axis)]
    psum x1 -> x0, blocking collectives: 129 us -> none  [local(): normal_flat, right_side = lax.psum((normal_flat, right_side), 'pix')]
    another operation x8 -> x0, other arithmetic: 72.8 us -> none  [the longest x4 70.5 us: whiten(): factor = jnp.linalg.cholesky(normal)]
    dot_general x11 -> x0, matrix products: 49.7 us -> none  [the longest x8 41.5 us: pick_rows(): jnp.dot(pose_hot, stack_rows, preferred_element_type=jnp.float32)]
    pallas_call x0 -> x10, Pallas kernels: none -> 34.9 us  [the longest x4 25.5 us: chunk_terms(): pl.pallas_call(functools.partial(chunk_kernel, fill), grid=(parts // ROWS...]
    ppermute x0 -> x22, starting transfers between devices: none -> 30.5 us  [the longest x20 20.3 us: hop(): return lax.ppermute(block, 'dom', perm)]
    all_to_all x0 -> x2, blocking collectives: none -> 29.3 us  [the longest x1 19.9 us: reduce_all(): spread = lax.all_to_all(spread, 'pix', 0, 0, axis_index_groups=CORE_GROUPS)]
    ppermute x0 -> x22, waiting for transfers between devices: none -> 22.2 us  [the longest x20 20.1 us: hop(): return lax.ppermute(block, 'dom', perm)]
  transfers between devices with their start and end apart: 9 -> 22, of which waited for: 9 -> 8; matrix products, arithmetic and copies ran while one was open for 2% -> 11% of each run, Pallas kernels for 0% -> 14%
where the time goes in v1:
time: 146 us; the launch traced here: 145 us
  Pallas kernels  34.9 us (24%)
  starting transfers between devices  30.5 us (21%)
  blocking collectives  29.3 us (20%)
  local copies, waits for them, and re-layouts  25.3 us (17%)
  waiting for transfers between devices  22.2 us (15%)
  other arithmetic  1.63 us (1%)
    pallas_call x4, Pallas kernels, chunk_terms(): pl.pallas_call(functools.partial(chunk_kernel, fill), grid=(parts // ROWS...  25.5 us
    unnamed x58, local copies, waits for them, and re-layouts  21.1 us
    ppermute x20, starting transfers between devices, hop(): return lax.ppermute(block, 'dom', perm)  20.3 us
    ppermute x20, waiting for transfers between devices, hop(): return lax.ppermute(block, 'dom', perm)  20.1 us
    all_to_all x1, blocking collectives, reduce_all(): spread = lax.all_to_all(spread, 'pix', 0, 0, axis_index_groups=CORE_GROUPS)  19.9 us
    all_to_all x1, blocking collectives, reduce_all(): spread = lax.all_to_all(spread, 'dom', 0, 0)  9.46 us
    ppermute x1, starting transfers between devices, reduce_all(): other = lax.ppermute(send, 'pix', CORE_SWAP)  6.72 us
    ppermute x1, starting transfers between devices, reduce_all(): other = lax.ppermute(own, 'pix', CORE_SWAP)  3.46 us
  transfers between devices with their start and end apart: 22, of which 8 were waited for; matrix products, arithmetic and copies ran while one was open for 11% of the time, Pallas kernels for 14%

profile of v1, /device:TPU:1, one launch (start us, length us, event | category | flops | bytes accessed | tf_op | source)
XLA Modules:
  0.0 144.8 jit_solution(16211928803711240432)
XLA Ops:
  0.6 1.5 %copy.19 = bf16[32,8,2,1024]{3,1,2,0:T(8,128)(2,1)S(1)} copy(bf16[32,8,2,1024]{3,2,1,0:T(2,128)(2,1)} %bitcast.29) | data formatting | bytes 2097152
  2.2 2.1 %collective-permute-start.10 = (bf16[256,512]{1,0:T(8,128)(2,1)S(1)}, bf16[256,512]{1,0:T(8,128)(2,1)S(1)}, u32[]{:S(2)}, u32[]{:S(2)}) collective-permute-start(bf16[256,512]{1,0:T(8,128)(2,1)S(1)} %pad_maximum_fusion.4), channel_id=1, source_target_pairs={{0,32},{32,0},{64,96},{96,64},{128,160},{160,128},{192,224},{224,1... | collective-permute-start | bytes 786440 | tf_op jit(solution)/shard_map/ppermute | solution.py:321
  5.1 1.3 collective-permute-start.15
  6.4 1.4 collective-permute-start.16
  8.6 2.7 %collective-permute-start.1 = (bf16[256,512]{1,0:T(8,128)(2,1)S(1)}, bf16[256,512]{1,0:T(8,128)(2,1)S(1)}, u32[]{:S(2)}, u32[]{:S(2)}) collective-permute-start(bf16[256,512]{1,0:T(8,128)(2,1)S(1)} %get-tuple-element.44), channel_id=1, source_target_pairs={{0,192},{32,224},{64,0},{96,32},{128,64},{160,96},{192,128},{224,1... | collective-permute-start | bytes 786440 | tf_op jit(solution)/shard_map/ppermute | solution.py:321
  11.7 1.3 collective-permute-done.15
  14.0 2.4 %collective-permute-start.12 = (bf16[512,512]{1,0:T(8,128)(2,1)S(1)}, bf16[512,512]{1,0:T(8,128)(2,1)S(1)}, u32[]{:S(2)}, u32[]{:S(2)}) collective-permute-start(bf16[512,512]{1,0:T(8,128)(2,1)S(1)} %pad_maximum_fusion.1.rest_0_), channel_id=1, source_target_pairs={{0,192},{32,224},{64,0},{96,32},{128,64},{160,96},{192,128},{224,1... | collective-permute-start | bytes 1572872 | tf_op jit(solution)/shard_map/ppermute | solution.py:321
  18.7 1.7 %collective-permute-start.18 = (bf16[128,512]{1,0:T(8,128)(2,1)S(1)}, bf16[128,512]{1,0:T(8,128)(2,1)S(1)}, u32[]{:S(2)}, u32[]{:S(2)}) collective-permute-start(bf16[128,512]{1,0:T(8,128)(2,1)S(1)} %slice.79), channel_id=1, source_target_pairs={{0,192},{32,224},{64,0},{96,32},{128,64},{160,96},{192,128},{224,1... | collective-permute-start | bytes 393224 | tf_op jit(solution)/shard_map/ppermute | solution.py:321
  21.9 10.8 %collective-permute-done.17 = bf16[128,512]{1,0:T(8,128)(2,1)S(1)} collective-permute-done((bf16[128,512]{1,0:T(8,128)(2,1)S(1)}, bf16[128,512]{1,0:T(8,128)(2,1)S(1)}, u32[]{:S(2)}, u32[]{:S(2)}) %collective-permute-start.17) | collective-permute-done | bytes 131104 | tf_op jit(solution)/shard_map/ppermute | solution.py:321
  32.7 1.7 %collective-permute-start.3 = (bf16[128,512]{1,0:T(8,128)(2,1)S(1)}, bf16[128,512]{1,0:T(8,128)(2,1)S(1)}, u32[]{:S(2)}, u32[]{:S(2)}) collective-permute-start(bf16[128,512]{1,0:T(8,128)(2,1)S(1)} %slice.67), channel_id=1, source_target_pairs={{0,192},{32,224},{64,0},{96,32},{128,64},{160,96},{192,128},{224,1... | collective-permute-start | bytes 393224 | tf_op jit(solution)/shard_map/ppermute | solution.py:321
  35.7 2.7 %collective-permute-start.7 = (bf16[512,512]{1,0:T(8,128)(2,1)S(1)}, bf16[512,512]{1,0:T(8,128)(2,1)S(1)}, u32[]{:S(2)}, u32[]{:S(2)}) collective-permute-start(bf16[512,512]{1,0:T(8,128)(2,1)S(1)} %pad_maximum_fusion.rest_0_), channel_id=1, source_target_pairs={{0,192},{32,224},{64,0},{96,32},{128,64},{160,96},{192,128},{224,1... | collective-permute-start | bytes 1572872 | tf_op jit(solution)/shard_map/ppermute | solution.py:321
  40.0 1.2 collective-permute-start.4
  42.1 4.0 %collective-permute-done.6.rest_1_ = bf16[512,512]{1,0:T(8,128)(2,1)S(1)} collective-permute-done((bf16[512,512]{1,0:T(8,128)(2,1)S(1)}, bf16[512,512]{1,0:T(8,128)(2,1)S(1)}, u32[]{:S(2)}, u32[]{:S(2)}) %collective-permute-start.6) | collective-permute-done | bytes 524320 | tf_op jit(solution)/shard_map/ppermute | solution.py:321
  47.0 1.2 collective-permute-done.7.rest_2_
  49.8 1.9 %collective-permute-done.13.rest_3_ = bf16[256,512]{1,0:T(8,128)(2,1)S(1)} collective-permute-done((bf16[256,512]{1,0:T(8,128)(2,1)S(1)}, bf16[256,512]{1,0:T(8,128)(2,1)S(1)}, u32[]{:S(2)}, u32[]{:S(2)}) %collective-permute-start.13) | collective-permute-done | bytes 262176 | tf_op jit(solution)/shard_map/ppermute | solution.py:321
  52.4 1.2 collective-permute-start.9
  54.2 5.6 %copy.18 = bf16[128,8,2,1024]{3,1,2,0:T(8,128)(2,1)} copy(bf16[128,8,2,1024]{3,2,1,0:T(2,128)(2,1)} %bitcast.27) | data formatting | bytes 8388608
  60.1 1.7 %hot_rows.1.hot_ref = bf16[1024,2048]{1,0:T(8,128)(2,1)S(1)} custom-call(s32[1]{0:T(128)} %bitcast.2.place, s32[8]{0:T(128)S(1)} %copy-done.18, s32[1024,1]{1,0:T(8,128)S(1)} %copy.11.class_ref, s32[1024,1]{1,0:T(8,128)S(1)} %copy.12.pose_ref), custom_call_target="tpu_custom_call" | custom-call | tf_op jit(solution)/shard_map/hot_rows/pallas_call | solution.py:64
  62.4 6.1 %chunk_terms.6 = (f32[96,64]{1,0:T(8,128)S(1)}, f32[2,1024]{1,0:T(2,128)S(1)}) custom-call(s32[1]{0:T(128)} %bitcast.7.first, bf16[1024,2048]{1,0:T(8,128)(2,1)S(1)} %hot_rows.1.hot_ref, bf16[1024,2048]{1,0:T(8,128)(2,1)S(1)} %bitcast.15, bf16[1024,2048]{1,0:T(8,128)(2,1)S(1)} %bitcast.16, f32[1024,1]{1,0:T(8,128)S(1)} %copy.13.defocus_ref, ...), custom_call_target="tpu_custom_call" | custom-call | flops 2147483648 | bytes 8388608 | tf_op jit(solution)/shard_map/chunk_terms/pallas_call | solution.py:180
  69.8 6.1 %chunk_terms.5 = (f32[96,64]{1,0:T(8,128)S(1)}, f32[2,1024]{1,0:T(2,128)S(1)}) custom-call(s32[1]{0:T(128)} %bitcast.6.first, bf16[1024,2048]{1,0:T(8,128)(2,1)S(1)} %hot_rows.1.hot_ref, bf16[1024,2048]{1,0:T(8,128)(2,1)S(1)} %bitcast.17, bf16[1024,2048]{1,0:T(8,128)(2,1)S(1)} %bitcast.18, f32[1024,1]{1,0:T(8,128)S(1)} %copy.13.defocus_ref, ...), custom_call_target="tpu_custom_call" | custom-call | flops 2147483648 | bytes 8388608 | tf_op jit(solution)/shard_map/chunk_terms/pallas_call | solution.py:180
  77.1 6.6 %chunk_terms.7 = (f32[96,64]{1,0:T(8,128)S(1)}, f32[2,1024]{1,0:T(2,128)S(1)}) custom-call(s32[1]{0:T(128)} %bitcast.8.first, bf16[1024,2048]{1,0:T(8,128)(2,1)S(1)} %hot_rows.1.hot_ref, bf16[1024,2048]{1,0:T(8,128)(2,1)S(1)} %bitcast.19, bf16[1024,2048]{1,0:T(8,128)(2,1)S(1)} %bitcast.20, f32[1024,1]{1,0:T(8,128)S(1)} %copy.13.defocus_ref, ...), custom_call_target="tpu_custom_call" | custom-call | flops 2147483648 | bytes 8388608 | tf_op jit(solution)/shard_map/chunk_terms/pallas_call | solution.py:180
  84.9 6.6 %chunk_terms.4 = (f32[96,64]{1,0:T(8,128)S(1)}, f32[2,1024]{1,0:T(2,128)S(1)}) custom-call(s32[1]{0:T(128)} %bitcast.1.first, bf16[1024,2048]{1,0:T(8,128)(2,1)S(1)} %hot_rows.1.hot_ref, bf16[1024,2048]{1,0:T(8,128)(2,1)S(1)} %bitcast.21, bf16[1024,2048]{1,0:T(8,128)(2,1)S(1)} %bitcast.22, f32[1024,1]{1,0:T(8,128)S(1)} %copy.13.defocus_ref, ...), custom_call_target="tpu_custom_call" | custom-call | flops 2147483648 | bytes 8388608 | tf_op jit(solution)/shard_map/chunk_terms/pallas_call | solution.py:180
  92.8 1.6 %pack.1 = (f32[32,128]{1,0:T(8,128)}, f32[32,128]{1,0:T(8,128)}) custom-call(s32[1]{0:T(128)} %bitcast.core, f32[96,64]{1,0:T(8,128)} %copy-done.13, f32[96,64]{1,0:T(8,128)} %copy-done.11, f32[96,64]{1,0:T(8,128)} %copy-done.10, f32[96,64]{1,0:T(8,128)} %copy-done.12, f32[2,1024]{1,0:T(2,128)} %copy-done.17, f32[2,1024]{1,0:T(2,128)} %copy-done.15, ...), custom_call_target="tpu_custom_call" | custom-call | tf_op jit(solution)/shard_map/pack/pallas_call | solution.py:285
  94.4 6.7 %collective-permute-start.20 = (f32[32,128]{1,0:T(8,128)}, f32[32,128]{1,0:T(8,128)S(1)}, u32[]{:S(2)}, u32[]{:S(2)}) collective-permute-start(f32[32,128]{1,0:T(8,128)} %get-tuple-element.25), channel_id=1, source_target_pairs={{0,1},{1,0},{2,3},{3,2},{4,5},{5,4},{6,7},{7,6},{8,9},{9,8},{10,11... | collective-permute-start | bytes 49160 | tf_op jit(solution)/shard_map/ppermute | solution.py:292
  102.7 1.4 spread_dom.1
  104.1 9.5 %all_to_all.10.in_ref = f32[8,24,128]{2,1,0:T(8,128)} all-to-all(f32[8,24,128]{2,1,0:T(8,128)} %get-tuple-element.26), channel_id=1, replica_groups=mesh['dom'=8,'pix'=32] {'dom'}, dimensions={0} | all-to-all | bytes 196608 | tf_op jit(solution)/shard_map/all_to_all | solution.py:298
  113.6 1.6 %spread_pix.1 = f32[16,32,128]{2,1,0:T(8,128)} custom-call(f32[8,24,128]{2,1,0:T(8,128)} %all_to_all.10.in_ref, f32[8,128]{1,0:T(8,128)} %get-tuple-element.27.grad_ref), custom_call_target="tpu_custom_call" | custom-call | tf_op jit(solution)/shard_map/spread_pix/pallas_call | solution.py:299
  115.2 19.9 %all_to_all.11.in_ref = f32[16,32,128]{2,1,0:T(8,128)} all-to-all(f32[16,32,128]{2,1,0:T(8,128)} %spread_pix.1), channel_id=1, replica_groups={{0,2,4,6,8,10,12,14,16,18,20,22,24,26,28,30},{1,3,5,7,9,11,13,15,17,19,..., dimensions={0} | all-to-all | bytes 524288 | tf_op jit(solution)/shard_map/all_to_all | solution.py:304
  135.1 1.6 %total.1.own_ref = f32[32,128]{1,0:T(8,128)} custom-call(f32[16,32,128]{2,1,0:T(8,128)} %all_to_all.11.in_ref), custom_call_target="tpu_custom_call" | custom-call | tf_op jit(solution)/shard_map/total/pallas_call | solution.py:305
  136.6 3.5 %collective-permute-start.21 = (f32[32,128]{1,0:T(8,128)}, f32[32,128]{1,0:T(8,128)S(1)}, u32[]{:S(2)}, u32[]{:S(2)}) collective-permute-start(f32[32,128]{1,0:T(8,128)} %total.1.own_ref), channel_id=1, source_target_pairs={{0,1},{1,0},{2,3},{3,2},{4,5},{5,4},{6,7},{7,6},{8,9},{9,8},{10,11... | collective-permute-start | bytes 49160 | tf_op jit(solution)/shard_map/ppermute | solution.py:306
  141.7 1.6 %whiten.1 = (f32[64,12]{1,0:T(8,128)}, f32[8,128]{1,0:T(8,128)}) custom-call(s32[1]{0:T(128)} %bitcast.core, f32[32,128]{1,0:T(8,128)} %total.1.own_ref, f32[32,128]{1,0:T(8,128)} %copy-done.20), custom_call_target="tpu_custom_call" | custom-call | tf_op jit(solution)/shard_map/whiten/pallas_call | solution.py:307
  143.3 1.4 copy.17
  (102 shorter events, 23.2 us)
Async XLA Ops:
  2.2 9.1 %collective-permute-start.10 = (bf16[256,512]{1,0:T(8,128)(2,1)S(1)}, bf16[256,512]{1,0:T(8,128)(2,1)S(1)}, u32[]{:S(2)}, u32[]{:S(2)}) collective-permute-start(bf16[256,512]{1,0:T(8,128)(2,1)S(1)} %pad_maximum_fusion.4), channel_id=1, source_target_pairs={{0,32},{32,0},{64,96},{96,64},{128,160},{160,128},{192,224},{224,1... | collective-permute-start | bytes 786440 | tf_op jit(solution)/shard_map/ppermute | solution.py:321
  5.1 7.9 %collective-permute-start.15 = (bf16[256,512]{1,0:T(8,128)(2,1)S(1)}, bf16[256,512]{1,0:T(8,128)(2,1)S(1)}, u32[]{:S(2)}, u32[]{:S(2)}) collective-permute-start(bf16[256,512]{1,0:T(8,128)(2,1)S(1)} %get-tuple-element.42), channel_id=1, source_target_pairs={{0,64},{32,96},{64,128},{96,160},{128,192},{160,224},{192,0},{224,... | collective-permute-start | bytes 786440 | tf_op jit(solution)/shard_map/ppermute | solution.py:321
  6.4 7.6 %collective-permute-start.16 = (bf16[256,512]{1,0:T(8,128)(2,1)S(1)}, bf16[256,512]{1,0:T(8,128)(2,1)S(1)}, u32[]{:S(2)}, u32[]{:S(2)}) collective-permute-start(bf16[256,512]{1,0:T(8,128)(2,1)S(1)} %get-tuple-element.42), channel_id=1, source_target_pairs={{0,192},{32,224},{64,0},{96,32},{128,64},{160,96},{192,128},{224,1... | collective-permute-start | bytes 786440 | tf_op jit(solution)/shard_map/ppermute | solution.py:321
  8.6 10.0 %collective-permute-start = (bf16[256,512]{1,0:T(8,128)(2,1)S(1)}, bf16[256,512]{1,0:T(8,128)(2,1)S(1)}, u32[]{:S(2)}, u32[]{:S(2)}) collective-permute-start(bf16[256,512]{1,0:T(8,128)(2,1)S(1)} %get-tuple-element.44), channel_id=1, source_target_pairs={{0,64},{32,96},{64,128},{96,160},{128,192},{160,224},{192,0},{224,... | collective-permute-start | bytes 786440 | tf_op jit(solution)/shard_map/ppermute | solution.py:321
  8.6 12.4 %collective-permute-start.1 = (bf16[256,512]{1,0:T(8,128)(2,1)S(1)}, bf16[256,512]{1,0:T(8,128)(2,1)S(1)}, u32[]{:S(2)}, u32[]{:S(2)}) collective-permute-start(bf16[256,512]{1,0:T(8,128)(2,1)S(1)} %get-tuple-element.44), channel_id=1, source_target_pairs={{0,192},{32,224},{64,0},{96,32},{128,64},{160,96},{192,128},{224,1... | collective-permute-start | bytes 786440 | tf_op jit(solution)/shard_map/ppermute | solution.py:321
  11.3 42.3 %copy-start.21 = (s32[1024,1]{0,1:T(1,128)S(1)}, s32[1024,1]{0,1:T(1,128)}, u32[]{:S(2)}) copy-start(s32[1024,1]{0,1:T(1,128)} %param.9) | copy-start | bytes 12292
  11.3 5.9 %collective-permute-start.5 = (bf16[256,512]{1,0:T(8,128)(2,1)S(1)}, bf16[256,512]{1,0:T(8,128)(2,1)S(1)}, u32[]{:S(2)}, u32[]{:S(2)}) collective-permute-start(bf16[256,512]{1,0:T(8,128)(2,1)S(1)} %pad_maximum_fusion.3), channel_id=1, source_target_pairs={{0,32},{32,0},{64,96},{96,64},{128,160},{160,128},{192,224},{224,1... | collective-permute-start | bytes 786440 | tf_op jit(solution)/shard_map/ppermute | solution.py:321
  11.7 42.2 %copy-start.22 = (s32[1024]{0:T(1024)S(1)}, s32[1024]{0:T(1024)}, u32[]{:S(2)}) copy-start(s32[1024]{0:T(1024)} %param.10) | copy-start | bytes 12292
  13.1 26.9 %collective-permute-start.11 = (bf16[512,512]{1,0:T(8,128)(2,1)S(1)}, bf16[512,512]{1,0:T(8,128)(2,1)S(1)}, u32[]{:S(2)}, u32[]{:S(2)}) collective-permute-start(bf16[512,512]{1,0:T(8,128)(2,1)S(1)} %pad_maximum_fusion.1.rest_0_), channel_id=1, source_target_pairs={{0,64},{32,96},{64,128},{96,160},{128,192},{160,224},{192,0},{224,... | collective-permute-start | bytes 1572872 | tf_op jit(solution)/shard_map/ppermute | solution.py:321
  14.0 27.2 %collective-permute-start.12 = (bf16[512,512]{1,0:T(8,128)(2,1)S(1)}, bf16[512,512]{1,0:T(8,128)(2,1)S(1)}, u32[]{:S(2)}, u32[]{:S(2)}) collective-permute-start(bf16[512,512]{1,0:T(8,128)(2,1)S(1)} %pad_maximum_fusion.1.rest_0_), channel_id=1, source_target_pairs={{0,192},{32,224},{64,0},{96,32},{128,64},{160,96},{192,128},{224,1... | collective-permute-start | bytes 1572872 | tf_op jit(solution)/shard_map/ppermute | solution.py:321
  17.2 15.5 %collective-permute-start.17 = (bf16[128,512]{1,0:T(8,128)(2,1)S(1)}, bf16[128,512]{1,0:T(8,128)(2,1)S(1)}, u32[]{:S(2)}, u32[]{:S(2)}) collective-permute-start(bf16[128,512]{1,0:T(8,128)(2,1)S(1)} %slice.78), channel_id=1, source_target_pairs={{0,64},{32,96},{64,128},{96,160},{128,192},{160,224},{192,0},{224,... | collective-permute-start | bytes 393224 | tf_op jit(solution)/shard_map/ppermute | solution.py:321
  18.7 16.4 %collective-permute-start.18 = (bf16[128,512]{1,0:T(8,128)(2,1)S(1)}, bf16[128,512]{1,0:T(8,128)(2,1)S(1)}, u32[]{:S(2)}, u32[]{:S(2)}) collective-permute-start(bf16[128,512]{1,0:T(8,128)(2,1)S(1)} %slice.79), channel_id=1, source_target_pairs={{0,192},{32,224},{64,0},{96,32},{128,64},{160,96},{192,128},{224,1... | collective-permute-start | bytes 393224 | tf_op jit(solution)/shard_map/ppermute | solution.py:321
  21.1 14.6 %collective-permute-start.2 = (bf16[128,512]{1,0:T(8,128)(2,1)S(1)}, bf16[128,512]{1,0:T(8,128)(2,1)S(1)}, u32[]{:S(2)}, u32[]{:S(2)}) collective-permute-start(bf16[128,512]{1,0:T(8,128)(2,1)S(1)} %slice.66), channel_id=1, source_target_pairs={{0,64},{32,96},{64,128},{96,160},{128,192},{160,224},{192,0},{224,... | collective-permute-start | bytes 393224 | tf_op jit(solution)/shard_map/ppermute | solution.py:321
  32.7 5.7 %collective-permute-start.3 = (bf16[128,512]{1,0:T(8,128)(2,1)S(1)}, bf16[128,512]{1,0:T(8,128)(2,1)S(1)}, u32[]{:S(2)}, u32[]{:S(2)}) collective-permute-start(bf16[128,512]{1,0:T(8,128)(2,1)S(1)} %slice.67), channel_id=1, source_target_pairs={{0,192},{32,224},{64,0},{96,32},{128,64},{160,96},{192,128},{224,1... | collective-permute-start | bytes 393224 | tf_op jit(solution)/shard_map/ppermute | solution.py:321
  35.1 11.1 %collective-permute-start.6 = (bf16[512,512]{1,0:T(8,128)(2,1)S(1)}, bf16[512,512]{1,0:T(8,128)(2,1)S(1)}, u32[]{:S(2)}, u32[]{:S(2)}) collective-permute-start(bf16[512,512]{1,0:T(8,128)(2,1)S(1)} %pad_maximum_fusion.rest_0_), channel_id=1, source_target_pairs={{0,64},{32,96},{64,128},{96,160},{128,192},{160,224},{192,0},{224,... | collective-permute-start | bytes 1572872 | tf_op jit(solution)/shard_map/ppermute | solution.py:321
  35.7 12.5 %collective-permute-start.7 = (bf16[512,512]{1,0:T(8,128)(2,1)S(1)}, bf16[512,512]{1,0:T(8,128)(2,1)S(1)}, u32[]{:S(2)}, u32[]{:S(2)}) collective-permute-start(bf16[512,512]{1,0:T(8,128)(2,1)S(1)} %pad_maximum_fusion.rest_0_), channel_id=1, source_target_pairs={{0,192},{32,224},{64,0},{96,32},{128,64},{160,96},{192,128},{224,1... | collective-permute-start | bytes 1572872 | tf_op jit(solution)/shard_map/ppermute | solution.py:321
  38.4 38.7 %collective-permute-start.19 = (bf16[1024,512]{1,0:T(8,128)(2,1)}, bf16[1024,512]{1,0:T(8,128)(2,1)}, u32[]{:S(2)}, u32[]{:S(2)}) collective-permute-start(bf16[1024,512]{1,0:T(8,128)(2,1)} %constant_dynamic-update-slice_fusion.5.rest_0_), channel_id=1, source_target_pairs={{0,32},{32,0},{64,96},{96,64},{128,160},{160,128},{192,224},{224,1... | collective-permute-start | bytes 3145736 | tf_op jit(solution)/shard_map/ppermute | solution.py:321
  40.0 45.0 %collective-permute-start.4 = (bf16[1024,512]{1,0:T(8,128)(2,1)}, bf16[1024,512]{1,0:T(8,128)(2,1)}, u32[]{:S(2)}, u32[]{:S(2)}) collective-permute-start(bf16[1024,512]{1,0:T(8,128)(2,1)} %constant_dynamic-update-slice_fusion.rest_0_), channel_id=1, source_target_pairs={{0,32},{32,0},{64,96},{96,64},{128,160},{160,128},{192,224},{224,1... | collective-permute-start | bytes 3145736 | tf_op jit(solution)/shard_map/ppermute | solution.py:321
  41.2 12.4 %copy-start.1 = (bf16[512,512]{1,0:T(8,128)(2,1)}, bf16[512,512]{1,0:T(8,128)(2,1)S(1)}, u32[]{:S(2)}) copy-start(bf16[512,512]{1,0:T(8,128)(2,1)S(1)} %collective-permute-done.12.rest_2_) | copy-start | bytes 1572868
  41.2 10.5 %collective-permute-start.13 = (bf16[256,512]{1,0:T(8,128)(2,1)S(1)}, bf16[256,512]{1,0:T(8,128)(2,1)S(1)}, u32[]{:S(2)}, u32[]{:S(2)}) collective-permute-start(bf16[256,512]{1,0:T(8,128)(2,1)S(1)} %slice.74), channel_id=1, source_target_pairs={{0,64},{32,96},{64,128},{96,160},{128,192},{160,224},{192,0},{224,... | collective-permute-start | bytes 786440 | tf_op jit(solution)/shard_map/ppermute | solution.py:321
  46.1 7.8 %copy-start.3 = (bf16[512,512]{1,0:T(8,128)(2,1)}, bf16[512,512]{1,0:T(8,128)(2,1)S(1)}, u32[]{:S(2)}) copy-start(bf16[512,512]{1,0:T(8,128)(2,1)S(1)} %collective-permute-done.6.rest_1_) | copy-start | bytes 1572868
  46.1 15.6 %collective-permute-start.14 = (bf16[256,512]{1,0:T(8,128)(2,1)}, bf16[256,512]{1,0:T(8,128)(2,1)}, u32[]{:S(2)}, u32[]{:S(2)}) collective-permute-start(bf16[256,512]{1,0:T(8,128)(2,1)} %slice.75), channel_id=1, source_target_pairs={{0,192},{32,224},{64,0},{96,32},{128,64},{160,96},{192,128},{224,1... | collective-permute-start | bytes 786440 | tf_op jit(solution)/shard_map/ppermute | solution.py:321
  48.2 21.5 %collective-permute-start.8 = (bf16[256,512]{1,0:T(8,128)(2,1)}, bf16[256,512]{1,0:T(8,128)(2,1)S(1)}, u32[]{:S(2)}, u32[]{:S(2)}) collective-permute-start(bf16[256,512]{1,0:T(8,128)(2,1)} %slice.70), channel_id=1, source_target_pairs={{0,64},{32,96},{64,128},{96,160},{128,192},{160,224},{192,0},{224,... | collective-permute-start | bytes 786440 | tf_op jit(solution)/shard_map/ppermute | solution.py:321
  52.4 17.3 %collective-permute-start.9 = (bf16[256,512]{1,0:T(8,128)(2,1)}, bf16[256,512]{1,0:T(8,128)(2,1)}, u32[]{:S(2)}, u32[]{:S(2)}) collective-permute-start(bf16[256,512]{1,0:T(8,128)(2,1)} %slice.71), channel_id=1, source_target_pairs={{0,192},{32,224},{64,0},{96,32},{128,64},{160,96},{192,128},{224,1... | collective-permute-start | bytes 786440 | tf_op jit(solution)/shard_map/ppermute | solution.py:321
  54.1 5.6 %copy-start.23 = (bf16[1024]{0:T(1024)(128)(2,1)S(1)}, bf16[1024]{0:T(1024)(128)(2,1)}, u32[]{:S(2)}) copy-start(bf16[1024]{0:T(1024)(128)(2,1)} %param.12) | copy-start | bytes 6148
  54.2 5.9 %copy-start.18 = (s32[8]{0:T(128)S(1)}, s32[8]{0:T(128)}, u32[]{:S(2)}) copy-start(s32[8]{0:T(128)} %slot_class.1) | copy-start | bytes 100
  60.0 2.3 %copy-start.2 = (bf16[512,512]{1,0:T(8,128)(2,1)S(1)}, bf16[512,512]{1,0:T(8,128)(2,1)}, u32[]{:S(2)}) copy-start(bf16[512,512]{1,0:T(8,128)(2,1)} %copy-done.1) | copy-start | bytes 1572868
  60.0 2.4 %copy-start.8 = (bf16[256,512]{1,0:T(8,128)(2,1)S(1)}, bf16[256,512]{1,0:T(8,128)(2,1)}, u32[]{:S(2)}) copy-start(bf16[256,512]{1,0:T(8,128)(2,1)} %copy-done.7) | copy-start | bytes 786436
  62.4 7.4 %copy-start.4 = (bf16[512,512]{1,0:T(8,128)(2,1)S(1)}, bf16[512,512]{1,0:T(8,128)(2,1)}, u32[]{:S(2)}) copy-start(bf16[512,512]{1,0:T(8,128)(2,1)} %copy-done.3) | copy-start | bytes 1572868
  62.4 7.4 %copy-start.6 = (bf16[512,512]{1,0:T(8,128)(2,1)S(1)}, bf16[512,512]{1,0:T(8,128)(2,1)}, u32[]{:S(2)}) copy-start(bf16[512,512]{1,0:T(8,128)(2,1)} %copy-done.5) | copy-start | bytes 1572868
  94.4 7.8 %collective-permute-start.20 = (f32[32,128]{1,0:T(8,128)}, f32[32,128]{1,0:T(8,128)S(1)}, u32[]{:S(2)}, u32[]{:S(2)}) collective-permute-start(f32[32,128]{1,0:T(8,128)} %get-tuple-element.25), channel_id=1, source_target_pairs={{0,1},{1,0},{2,3},{3,2},{4,5},{5,4},{6,7},{7,6},{8,9},{9,8},{10,11... | collective-permute-start | bytes 49160 | tf_op jit(solution)/shard_map/ppermute | solution.py:292
  136.6 4.5 %collective-permute-start.21 = (f32[32,128]{1,0:T(8,128)}, f32[32,128]{1,0:T(8,128)S(1)}, u32[]{:S(2)}, u32[]{:S(2)}) collective-permute-start(f32[32,128]{1,0:T(8,128)} %total.1.own_ref), channel_id=1, source_target_pairs={{0,1},{1,0},{2,3},{3,2},{4,5},{5,4},{6,7},{7,6},{8,9},{9,8},{10,11... | collective-permute-start | bytes 49160 | tf_op jit(solution)/shard_map/ppermute | solution.py:306
  (14 other events, 11.7 us)
